TPU v7x, 256 devices: a whole 4x4x8 slice. The times are simulated.
256 devices in a mesh: row: 16 (over z_lo, y), col: 16 (over x, z_hi, core).
Axes of the slice: x: 4, y: 4, z: 8 (z_hi: 2, z_lo: 4; z = z_hi * 4 + z_lo), core: 2. Of those that a mesh axis runs over, the one named last changes fastest.
Arguments:
- rhs: float32 [262144, 256], P(('row', 'col')), may hold values from -6 to 6
- local_mat: bfloat16 [262144, 1024], P(('row', 'col')), may hold values from -1 to 5
- local_inv: bfloat16 [262144, 1024], P(('row', 'col')), may hold values from -1 to 1
- basis_t: bfloat16 [24576, 1024], P(('row', 'col')), may hold values from -0.1875 to 0.1875
- coarse_inv: bfloat16 [24576, 24576], P('col', 'row'), may hold values from -0.0390625 to 0.0390625
- couple: float32 [256, 4, 128], P(('row', 'col')), may hold values from 0.5 to 2
- margin_rows: int32 [256, 4, 128], P(('row', 'col')), may hold values from 0 to 1023, as said below
Outputs:
- solution: float32 [262144, 256], P(('row', 'col'))
- residual: float32 [262144, 256], P(('row', 'col'))
Inputs may be any that keep to these rules, and one draw needn't show every extreme that they name: `margin_rows`: within each subdomain the 512 listed rows are all different.
All inputs are finite; a program needn't handle non-finite values.
Results may differ from a plain program's by a relative error of at most 0.024.
Values may be sent and summed in bfloat16 or wider, within the bound.
A program may use at most 64 MiB of HBM per device.

v0:
```python
import jax
import jax.numpy as jnp
from jax import lax
from jax.sharding import PartitionSpec as P

STEPS = 2


def padded(cells, sides, width):
    for axis, dim in sides:
        count = lax.axis_size(axis)
        ends = count - 1
        head = lax.slice_in_dim(cells, 0, width, axis=dim)
        tail = lax.slice_in_dim(cells, cells.shape[dim] - width, cells.shape[dim], axis=dim)
        cells = jnp.concatenate(
            [
                lax.ppermute(tail, axis, [(i, (i + 1) % count) for i in range(ends)]),
                cells,
                lax.ppermute(head, axis, [((i + 1) % count, i) for i in range(ends)]),
            ],
            axis=dim,
        )
    return cells


def laid_out(pieces, dim):
    pieces = jnp.moveaxis(pieces, 0, dim)
    dims = pieces.shape
    return pieces.reshape(*dims[:dim], dims[dim] * dims[dim + 1], *dims[dim + 2 :])


def sent_to_all(x, axis):
    size = lax.axis_size(axis)
    return lax.all_to_all(jnp.broadcast_to(x[None], (size, *x.shape)), axis, 0, 0, tiled=True)


def collect(x, axis, dim):
    return laid_out(sent_to_all(x, axis), dim)


def in_blocks(x, dim, size):
    before, after = (x.shape[:dim], x.shape[dim + 1 :])
    return jnp.moveaxis(x.reshape(*before, size, -1, *after), dim, 0)


def sum_at_owner(x, axis, dim):
    pieces = in_blocks(x, dim, lax.axis_size(axis))
    arrived = lax.all_to_all(pieces, axis, split_axis=0, concat_axis=0, tiled=True)
    return arrived.sum(axis=0)


def per_device(rhs, local_mat, local_inv, basis_t, coarse_inv, couple, margin_rows):
    face_index = margin_rows[0]
    flat_rows = face_index.reshape(-1)
    weights = couple[0]
    columns = rhs.shape[1]

    def neighbour_faces(vector_b):
        face_vals = vector_b[face_index]
        north_south = padded(face_vals[0:2], (("row", 0),), 1)
        west_east = padded(face_vals[2:4], (("col", 0),), 1)
        received = jnp.stack([north_south[0], north_south[3], west_east[0], west_east[3]])
        return received

    def apply_operator(vector):
        vector_b = vector.astype(jnp.bfloat16)
        received = neighbour_faces(vector_b)
        coupling_terms = (weights[:, :, None] * received.astype(jnp.float32)).reshape(-1, columns)
        coupled = jnp.zeros(vector.shape, jnp.float32).at[flat_rows].add(coupling_terms)
        return jnp.dot(local_mat, vector_b, preferred_element_type=jnp.float32) - coupled

    solution = jnp.zeros(rhs.shape, jnp.float32)
    residual = rhs
    for sweep in range(STEPS):
        if sweep > 0:
            residual = rhs - apply_operator(solution)
        rounded = residual.astype(jnp.bfloat16)
        restricted = jnp.dot(basis_t, rounded, preferred_element_type=jnp.float32).astype(
            jnp.bfloat16
        )
        gathered = collect(restricted, "col", 0)
        coarse_part = sum_at_owner(
            jnp.dot(coarse_inv, gathered, preferred_element_type=jnp.float32), "row", 0
        )
        coarse_b = coarse_part.astype(jnp.bfloat16)
        solution = solution + lax.dot_general(
            basis_t, coarse_b, (((0,), (0,)), ((), ())), preferred_element_type=jnp.float32
        )
        residual = rhs - apply_operator(solution)
        solution = solution + jnp.dot(
            local_inv, residual.astype(jnp.bfloat16), preferred_element_type=jnp.float32
        )
    residual = rhs - apply_operator(solution)
    return (solution, residual)


def solution(mesh):
    placed = (
        P(("row", "col"), None),
        P(("row", "col"), None),
        P(("row", "col"), None),
        P(("row", "col"), None),
        P("col", "row"),
        P(("row", "col"), None, None),
        P(("row", "col"), None, None),
    )
    return jax.shard_map(
        per_device,
        mesh=mesh,
        in_specs=placed,
        out_specs=(P(("row", "col"), None), P(("row", "col"), None)),
        check_vma=False,
    )
```

profile of v0, /device:TPU:34, one launch (start us, length us, event | category | flops | bytes accessed | tf_op | source)
XLA Modules:
  0.0 329.0 jit_solution(613726169375708921)
XLA Ops:
  2.4 33.8 %all_to_all.20 = bf16[16,96,256]{2,1,0:T(8,128)(2,1)S(1)} all-to-all(bf16[16,96,256]{2,1,0:T(8,128)(2,1)S(1)} %broadcast_in_dim.4), channel_id=1, replica_groups=mesh['row'=16,'col'=16] {'col'}, dimensions={0} | all-to-all | bytes 1572864 | tf_op jit(solution)/shard_map/all_to_all | solution.py:34
  36.2 4.9 %convolution_bitcast_fusion.1 = f32[1536,256]{0,1:T(8,128)} fusion(bf16[1536,256]{1,0:T(8,128)(2,1)S(1)} %bitcast.130, bf16[1536,1536]{1,0:T(8,128)(2,1)} %param.11), kind=kOutput, calls=%fused_computation.9 | convolution fusion | flops 1207959552 | bytes 7077888 | tf_op jit(solution)/shard_map/dot_general | solution.py:83
  41.1 3.0 copy.23
  44.2 6.5 %all-to-all-start.1 = ((f32[16,96,256]{2,1,0:T(8,128)}), f32[16,96,256]{2,1,0:T(8,128)}, u32[]{:S(2)}, u32[]{:S(2)}) async-start(f32[16,96,256]{2,1,0:T(8,128)} %bitcast.124), calls=%async_computation.1 | async-start | bytes 3145728 | tf_op jit(solution)/shard_map/all_to_all | solution.py:48
  50.7 37.1 %all-to-all-done.1 = f32[16,96,256]{2,1,0:T(8,128)} async-done(((f32[16,96,256]{2,1,0:T(8,128)}), f32[16,96,256]{2,1,0:T(8,128)}, u32[]{:S(2)}, u32[]{:S(2)}) %all-to-all-start.1) | async-done | bytes 1572896 | tf_op jit(solution)/shard_map/all_to_all | solution.py:48
  92.9 3.4 %gather_fusion = bf16[512,256]{1,0:T(8,128)(2,1)} fusion(bf16[1024,256]{1,0:T(8,128)(2,1)} %copy.24, s32[1024]{0:T(1024)S(1)} %pad_clamp_fusion), kind=kCustom, calls=%fused_computation | custom fusion | bytes 526336 | tf_op jit(solution)/shard_map/gather | solution.py:59
  101.3 5.8 %collective-permute-start.1 = (bf16[1,128,256]{2,1,0:T(8,128)(2,1)S(1)}, bf16[1,128,256]{2,1,0:T(8,128)(2,1)S(1)}, u32[]{:S(2)}, u32[]{:S(2)}) collective-permute-start(bf16[1,128,256]{2,1,0:T(8,128)(2,1)S(1)} %get-tuple-element.20), channel_id=1, source_target_pairs={{16,0},{32,16},{48,32},{64,48},{80,64},{96,80},{112,96},{128,112},... | collective-permute-start | bytes 196616 | tf_op jit(solution)/shard_map/ppermute | solution.py:19
  107.1 8.2 %collective-permute-start.3 = (bf16[1,128,256]{2,1,0:T(8,128)(2,1)S(1)}, bf16[1,128,256]{2,1,0:T(8,128)(2,1)S(1)}, u32[]{:S(2)}, u32[]{:S(2)}) collective-permute-start(bf16[1,128,256]{2,1,0:T(8,128)(2,1)S(1)} %get-tuple-element.21), channel_id=1, source_target_pairs={{1,0},{2,1},{3,2},{4,3},{5,4},{6,5},{7,6},{8,7},{9,8},{10,9},{11,1... | collective-permute-start | bytes 196616 | tf_op jit(solution)/shard_map/ppermute | solution.py:19
  117.9 4.8 %scatter_custom_fusion = f32[1024,256]{1,0:T(8,128)} fusion(s32[512]{0:T(512)S(1)} %bitcast.137, bf16[512,256]{1,0:T(8,128)(2,1)} %bitcast.127, f32[]{:T(128)} %constant.3.clone.1, f32[512]{0:T(512)S(1)} %bitcast.132), kind=kCustom, calls=%fused_computation.40 | custom fusion | flops 393216 | bytes 1312772 | tf_op jit(solution)/shard_map/scatter-add | solution.py:69
  122.7 5.8 %convolution_add_fusion.2 = f32[256,1024]{1,0:T(8,128)} fusion(f32[256,1024]{1,0:T(8,128)} %copy-done.4, bf16[1024,1024]{1,0:T(8,128)(2,1)} %param.9, f32[1024,256]{1,0:T(8,128)S(1)} %copy-done.1, f32[1024,256]{1,0:T(8,128)} %scatter_custom_fusion, bf16[1024,1024]{1,0:T(8,128)(2,1)S(1)} %copy-done), kind=kOutput, calls=%fused_computation.25 | convolution fusion | flops 1075052544 | bytes 8388608 | tf_op jit(solution)/shard_map/dot_general | solution.py:90
  132.7 3.3 %gather_fusion.1 = bf16[512,256]{1,0:T(8,128)(2,1)} fusion(bf16[1024,256]{1,0:T(8,128)(2,1)} %copy.25, s32[1024]{0:T(1024)S(1)} %pad_clamp_fusion), kind=kCustom, calls=%fused_computation.1 | custom fusion | bytes 526336 | tf_op jit(solution)/shard_map/gather | solution.py:59
  138.9 2.6 collective-permute-start.6
  141.5 5.8 %collective-permute-start.5 = (bf16[1,128,256]{2,1,0:T(8,128)(2,1)S(1)}, bf16[1,128,256]{2,1,0:T(8,128)(2,1)S(1)}, u32[]{:S(2)}, u32[]{:S(2)}) collective-permute-start(bf16[1,128,256]{2,1,0:T(8,128)(2,1)S(1)} %get-tuple-element.16), channel_id=1, source_target_pairs={{16,0},{32,16},{48,32},{64,48},{80,64},{96,80},{112,96},{128,112},... | collective-permute-start | bytes 196616 | tf_op jit(solution)/shard_map/ppermute | solution.py:19
  147.2 8.0 %collective-permute-start.7 = (bf16[1,128,256]{2,1,0:T(8,128)(2,1)S(1)}, bf16[1,128,256]{2,1,0:T(8,128)(2,1)S(1)}, u32[]{:S(2)}, u32[]{:S(2)}) collective-permute-start(bf16[1,128,256]{2,1,0:T(8,128)(2,1)S(1)} %get-tuple-element.17), channel_id=1, source_target_pairs={{1,0},{2,1},{3,2},{4,3},{5,4},{6,5},{7,6},{8,7},{9,8},{10,9},{11,1... | collective-permute-start | bytes 196616 | tf_op jit(solution)/shard_map/ppermute | solution.py:19
  158.3 4.8 %scatter_custom_fusion.1 = f32[1024,256]{1,0:T(8,128)} fusion(s32[512]{0:T(512)S(1)} %bitcast.138, bf16[512,256]{1,0:T(8,128)(2,1)} %bitcast.128, f32[]{:T(128)} %constant.3.clone.1, f32[512]{0:T(512)S(1)} %bitcast.133), kind=kCustom, calls=%fused_computation.38 | custom fusion | flops 393216 | bytes 1312772 | tf_op jit(solution)/shard_map/scatter-add | solution.py:69
  163.1 2.6 fusion.14
  165.7 33.8 %all_to_all.21 = bf16[16,96,256]{2,1,0:T(8,128)(2,1)S(1)} all-to-all(bf16[16,96,256]{2,1,0:T(8,128)(2,1)S(1)} %broadcast_in_dim.5), channel_id=1, replica_groups=mesh['row'=16,'col'=16] {'col'}, dimensions={0} | all-to-all | bytes 1572864 | tf_op jit(solution)/shard_map/all_to_all | solution.py:34
  199.5 4.9 %convolution_bitcast_fusion = f32[1536,256]{0,1:T(8,128)} fusion(bf16[1536,256]{1,0:T(8,128)(2,1)S(1)} %bitcast.131, bf16[1536,1536]{1,0:T(8,128)(2,1)} %param.11), kind=kOutput, calls=%fused_computation.8 | convolution fusion | flops 1207959552 | bytes 7077888 | tf_op jit(solution)/shard_map/dot_general | solution.py:83
  204.4 3.0 copy.26
  207.5 40.9 %all_to_all.22 = f32[16,96,256]{2,1,0:T(8,128)} all-to-all(f32[16,96,256]{2,1,0:T(8,128)} %bitcast.125), channel_id=1, replica_groups=mesh['row'=16,'col'=16] {'row'}, dimensions={0} | all-to-all | bytes 3145728 | tf_op jit(solution)/shard_map/all_to_all | solution.py:48
  255.3 2.7 gather_fusion.2
  262.1 5.8 %collective-permute-start.9 = (bf16[1,128,256]{2,1,0:T(8,128)(2,1)S(1)}, bf16[1,128,256]{2,1,0:T(8,128)(2,1)S(1)}, u32[]{:S(2)}, u32[]{:S(2)}) collective-permute-start(bf16[1,128,256]{2,1,0:T(8,128)(2,1)S(1)} %get-tuple-element.12), channel_id=1, source_target_pairs={{16,0},{32,16},{48,32},{64,48},{80,64},{96,80},{112,96},{128,112},... | collective-permute-start | bytes 196616 | tf_op jit(solution)/shard_map/ppermute | solution.py:19
  267.9 8.2 %collective-permute-start.11 = (bf16[1,128,256]{2,1,0:T(8,128)(2,1)S(1)}, bf16[1,128,256]{2,1,0:T(8,128)(2,1)S(1)}, u32[]{:S(2)}, u32[]{:S(2)}) collective-permute-start(bf16[1,128,256]{2,1,0:T(8,128)(2,1)S(1)} %get-tuple-element.13), channel_id=1, source_target_pairs={{1,0},{2,1},{3,2},{4,3},{5,4},{6,5},{7,6},{8,7},{9,8},{10,9},{11,1... | collective-permute-start | bytes 196616 | tf_op jit(solution)/shard_map/ppermute | solution.py:19
  278.2 4.4 %scatter_custom_fusion.2 = f32[1024,256]{1,0:T(8,128)} fusion(s32[512]{0:T(512)S(1)} %bitcast.139, bf16[512,256]{1,0:T(8,128)(2,1)S(1)} %bitcast.129, f32[]{:T(128)} %constant.3.clone.1, f32[512]{0:T(512)S(1)} %bitcast.134), kind=kCustom, calls=%fused_computation.36 | custom fusion | flops 393216 | bytes 1312772 | tf_op jit(solution)/shard_map/scatter-add | solution.py:69
  282.6 6.0 %fusion.38 = (bf16[1024,256]{0,1:T(8,128)(2,1)}, f32[1024,256]{0,1:T(8,128)}) fusion(f32[256,1024]{1,0:T(8,128)} %copy-done.2, bf16[1024,1024]{1,0:T(8,128)(2,1)} %param.9, f32[1024,256]{1,0:T(8,128)S(1)} %copy-done.1, f32[1024,256]{1,0:T(8,128)} %scatter_custom_fusion.2, bf16[1024,1024]{1,0:T(8,128)(2,1)S(1)} %copy-done), kind=kOutput, calls=%fused_computation.83 | convolution fusion | flops 1075314688 | bytes 8912896 | tf_op jit(solution)/shard_map/dot_general | solution.py:90
  290.7 2.7 gather_fusion.3
  295.9 2.6 collective-permute-start.14
  298.6 5.8 %collective-permute-start.13 = (bf16[1,128,256]{2,1,0:T(8,128)(2,1)S(1)}, bf16[1,128,256]{2,1,0:T(8,128)(2,1)S(1)}, u32[]{:S(2)}, u32[]{:S(2)}) collective-permute-start(bf16[1,128,256]{2,1,0:T(8,128)(2,1)S(1)} %get-tuple-element.8), channel_id=1, source_target_pairs={{16,0},{32,16},{48,32},{64,48},{80,64},{96,80},{112,96},{128,112},... | collective-permute-start | bytes 196616 | tf_op jit(solution)/shard_map/ppermute | solution.py:19
  304.3 8.0 %collective-permute-start.15 = (bf16[1,128,256]{2,1,0:T(8,128)(2,1)S(1)}, bf16[1,128,256]{2,1,0:T(8,128)(2,1)S(1)}, u32[]{:S(2)}, u32[]{:S(2)}) collective-permute-start(bf16[1,128,256]{2,1,0:T(8,128)(2,1)S(1)} %get-tuple-element.9), channel_id=1, source_target_pairs={{1,0},{2,1},{3,2},{4,3},{5,4},{6,5},{7,6},{8,7},{9,8},{10,9},{11,1... | collective-permute-start | bytes 196616 | tf_op jit(solution)/shard_map/ppermute | solution.py:19
  316.2 4.5 %scatter_custom_fusion.3 = f32[1024,256]{1,0:T(8,128)} fusion(s32[512]{0:T(512)S(1)} %bitcast.140, bf16[512,256]{1,0:T(8,128)(2,1)S(1)} %bitcast.126, f32[]{:T(128)} %constant.3.clone.1, f32[512]{0:T(512)S(1)} %bitcast.135), kind=kCustom, calls=%fused_computation.34 | custom fusion | flops 393216 | bytes 1312772 | tf_op jit(solution)/shard_map/scatter-add | solution.py:69
  320.7 2.5 copy.29
  323.2 3.3 fusion.7
  (66 shorter events, 48.8 us)
Async XLA Ops:
  0.6 122.1 %copy-start = (bf16[1024,1024]{1,0:T(8,128)(2,1)S(1)}, bf16[1024,1024]{1,0:T(8,128)(2,1)}, u32[]{:S(2)}) copy-start(bf16[1024,1024]{1,0:T(8,128)(2,1)} %param.8) | copy-start | bytes 6291460
  44.2 6.5 %copy-start.7 = (s32[1,4,128]{2,1,0:T(4,128)S(1)}, s32[1,4,128]{2,1,0:T(4,128)}, u32[]{:S(2)}) copy-start(s32[1,4,128]{2,1,0:T(4,128)} %param.13) | copy-start | bytes 6148
  44.2 45.2 %copy-start.5 = (bf16[96,1024]{1,0:T(8,128)(2,1)S(1)}, bf16[96,1024]{1,0:T(8,128)(2,1)}, u32[]{:S(2)}) copy-start(bf16[96,1024]{1,0:T(8,128)(2,1)} %param.10) | copy-start | bytes 589828
  44.2 43.7 %all-to-all-start.1 = ((f32[16,96,256]{2,1,0:T(8,128)}), f32[16,96,256]{2,1,0:T(8,128)}, u32[]{:S(2)}, u32[]{:S(2)}) async-start(f32[16,96,256]{2,1,0:T(8,128)} %bitcast.124), calls=%async_computation.1 | async-start | bytes 3145728 | tf_op jit(solution)/shard_map/all_to_all | solution.py:48
  89.7 1.1 copy-start.4
  90.8 27.1 %copy-start.6 = (f32[1,4,128]{2,1,0:T(4,128)S(1)}, f32[1,4,128]{2,1,0:T(4,128)}, u32[]{:S(2)}) copy-start(f32[1,4,128]{2,1,0:T(4,128)} %param.12) | copy-start | bytes 6148
  92.9 29.9 %copy-start.1 = (f32[1024,256]{1,0:T(8,128)S(1)}, f32[1024,256]{1,0:T(8,128)}, u32[]{:S(2)}) copy-start(f32[1024,256]{1,0:T(8,128)} %param.7) | copy-start | bytes 3145732
  97.2 18.1 %collective-permute-start = (bf16[1,128,256]{2,1,0:T(8,128)(2,1)S(1)}, bf16[1,128,256]{2,1,0:T(8,128)(2,1)S(1)}, u32[]{:S(2)}, u32[]{:S(2)}) collective-permute-start(bf16[1,128,256]{2,1,0:T(8,128)(2,1)S(1)} %get-tuple-element.18), channel_id=1, source_target_pairs={{0,16},{16,32},{32,48},{48,64},{64,80},{80,96},{96,112},{112,128},... | collective-permute-start | bytes 196616 | tf_op jit(solution)/shard_map/ppermute | solution.py:17
  99.4 15.9 %collective-permute-start.2 = (bf16[1,128,256]{2,1,0:T(8,128)(2,1)S(1)}, bf16[1,128,256]{2,1,0:T(8,128)(2,1)S(1)}, u32[]{:S(2)}, u32[]{:S(2)}) collective-permute-start(bf16[1,128,256]{2,1,0:T(8,128)(2,1)S(1)} %get-tuple-element.19), channel_id=1, source_target_pairs={{0,1},{1,2},{2,3},{3,4},{4,5},{5,6},{6,7},{7,8},{8,9},{9,10},{10,1... | collective-permute-start | bytes 196616 | tf_op jit(solution)/shard_map/ppermute | solution.py:17
  101.3 14.0 %collective-permute-start.1 = (bf16[1,128,256]{2,1,0:T(8,128)(2,1)S(1)}, bf16[1,128,256]{2,1,0:T(8,128)(2,1)S(1)}, u32[]{:S(2)}, u32[]{:S(2)}) collective-permute-start(bf16[1,128,256]{2,1,0:T(8,128)(2,1)S(1)} %get-tuple-element.20), channel_id=1, source_target_pairs={{16,0},{32,16},{48,32},{64,48},{80,64},{96,80},{112,96},{128,112},... | collective-permute-start | bytes 196616 | tf_op jit(solution)/shard_map/ppermute | solution.py:19
  107.1 10.1 %collective-permute-start.3 = (bf16[1,128,256]{2,1,0:T(8,128)(2,1)S(1)}, bf16[1,128,256]{2,1,0:T(8,128)(2,1)S(1)}, u32[]{:S(2)}, u32[]{:S(2)}) collective-permute-start(bf16[1,128,256]{2,1,0:T(8,128)(2,1)S(1)} %get-tuple-element.21), channel_id=1, source_target_pairs={{1,0},{2,1},{3,2},{4,3},{5,4},{6,5},{7,6},{8,7},{9,8},{10,9},{11,1... | collective-permute-start | bytes 196616 | tf_op jit(solution)/shard_map/ppermute | solution.py:19
  136.9 18.3 %collective-permute-start.4 = (bf16[1,128,256]{2,1,0:T(8,128)(2,1)S(1)}, bf16[1,128,256]{2,1,0:T(8,128)(2,1)S(1)}, u32[]{:S(2)}, u32[]{:S(2)}) collective-permute-start(bf16[1,128,256]{2,1,0:T(8,128)(2,1)S(1)} %get-tuple-element.14), channel_id=1, source_target_pairs={{0,16},{16,32},{32,48},{48,64},{64,80},{80,96},{96,112},{112,128},... | collective-permute-start | bytes 196616 | tf_op jit(solution)/shard_map/ppermute | solution.py:17
  138.9 16.3 %collective-permute-start.6 = (bf16[1,128,256]{2,1,0:T(8,128)(2,1)S(1)}, bf16[1,128,256]{2,1,0:T(8,128)(2,1)S(1)}, u32[]{:S(2)}, u32[]{:S(2)}) collective-permute-start(bf16[1,128,256]{2,1,0:T(8,128)(2,1)S(1)} %get-tuple-element.15), channel_id=1, source_target_pairs={{0,1},{1,2},{2,3},{3,4},{4,5},{5,6},{6,7},{7,8},{8,9},{9,10},{10,1... | collective-permute-start | bytes 196616 | tf_op jit(solution)/shard_map/ppermute | solution.py:17
  141.5 13.8 %collective-permute-start.5 = (bf16[1,128,256]{2,1,0:T(8,128)(2,1)S(1)}, bf16[1,128,256]{2,1,0:T(8,128)(2,1)S(1)}, u32[]{:S(2)}, u32[]{:S(2)}) collective-permute-start(bf16[1,128,256]{2,1,0:T(8,128)(2,1)S(1)} %get-tuple-element.16), channel_id=1, source_target_pairs={{16,0},{32,16},{48,32},{64,48},{80,64},{96,80},{112,96},{128,112},... | collective-permute-start | bytes 196616 | tf_op jit(solution)/shard_map/ppermute | solution.py:19
  147.2 10.3 %collective-permute-start.7 = (bf16[1,128,256]{2,1,0:T(8,128)(2,1)S(1)}, bf16[1,128,256]{2,1,0:T(8,128)(2,1)S(1)}, u32[]{:S(2)}, u32[]{:S(2)}) collective-permute-start(bf16[1,128,256]{2,1,0:T(8,128)(2,1)S(1)} %get-tuple-element.17), channel_id=1, source_target_pairs={{1,0},{2,1},{3,2},{4,3},{5,4},{6,5},{7,6},{8,7},{9,8},{10,9},{11,1... | collective-permute-start | bytes 196616 | tf_op jit(solution)/shard_map/ppermute | solution.py:19
  251.4 1.0 copy-start.2
  258.0 18.1 %collective-permute-start.8 = (bf16[1,128,256]{2,1,0:T(8,128)(2,1)S(1)}, bf16[1,128,256]{2,1,0:T(8,128)(2,1)S(1)}, u32[]{:S(2)}, u32[]{:S(2)}) collective-permute-start(bf16[1,128,256]{2,1,0:T(8,128)(2,1)S(1)} %get-tuple-element.10), channel_id=1, source_target_pairs={{0,16},{16,32},{32,48},{48,64},{64,80},{80,96},{96,112},{112,128},... | collective-permute-start | bytes 196616 | tf_op jit(solution)/shard_map/ppermute | solution.py:17
  260.1 15.9 %collective-permute-start.10 = (bf16[1,128,256]{2,1,0:T(8,128)(2,1)S(1)}, bf16[1,128,256]{2,1,0:T(8,128)(2,1)S(1)}, u32[]{:S(2)}, u32[]{:S(2)}) collective-permute-start(bf16[1,128,256]{2,1,0:T(8,128)(2,1)S(1)} %get-tuple-element.11), channel_id=1, source_target_pairs={{0,1},{1,2},{2,3},{3,4},{4,5},{5,6},{6,7},{7,8},{8,9},{9,10},{10,1... | collective-permute-start | bytes 196616 | tf_op jit(solution)/shard_map/ppermute | solution.py:17
  262.1 14.0 %collective-permute-start.9 = (bf16[1,128,256]{2,1,0:T(8,128)(2,1)S(1)}, bf16[1,128,256]{2,1,0:T(8,128)(2,1)S(1)}, u32[]{:S(2)}, u32[]{:S(2)}) collective-permute-start(bf16[1,128,256]{2,1,0:T(8,128)(2,1)S(1)} %get-tuple-element.12), channel_id=1, source_target_pairs={{16,0},{32,16},{48,32},{64,48},{80,64},{96,80},{112,96},{128,112},... | collective-permute-start | bytes 196616 | tf_op jit(solution)/shard_map/ppermute | solution.py:19
  267.9 10.3 %collective-permute-start.11 = (bf16[1,128,256]{2,1,0:T(8,128)(2,1)S(1)}, bf16[1,128,256]{2,1,0:T(8,128)(2,1)S(1)}, u32[]{:S(2)}, u32[]{:S(2)}) collective-permute-start(bf16[1,128,256]{2,1,0:T(8,128)(2,1)S(1)} %get-tuple-element.13), channel_id=1, source_target_pairs={{1,0},{2,1},{3,2},{4,3},{5,4},{6,5},{7,6},{8,7},{9,8},{10,9},{11,1... | collective-permute-start | bytes 196616 | tf_op jit(solution)/shard_map/ppermute | solution.py:19
  294.0 22.1 %collective-permute-start.12 = (bf16[1,128,256]{2,1,0:T(8,128)(2,1)}, bf16[1,128,256]{2,1,0:T(8,128)(2,1)S(1)}, u32[]{:S(2)}, u32[]{:S(2)}) collective-permute-start(bf16[1,128,256]{2,1,0:T(8,128)(2,1)} %get-tuple-element.6), channel_id=1, source_target_pairs={{0,16},{16,32},{32,48},{48,64},{64,80},{80,96},{96,112},{112,128},... | collective-permute-start | bytes 196616 | tf_op jit(solution)/shard_map/ppermute | solution.py:17
  295.9 20.2 %collective-permute-start.14 = (bf16[1,128,256]{2,1,0:T(8,128)(2,1)}, bf16[1,128,256]{2,1,0:T(8,128)(2,1)S(1)}, u32[]{:S(2)}, u32[]{:S(2)}) collective-permute-start(bf16[1,128,256]{2,1,0:T(8,128)(2,1)} %get-tuple-element.7), channel_id=1, source_target_pairs={{0,1},{1,2},{2,3},{3,4},{4,5},{5,6},{6,7},{7,8},{8,9},{9,10},{10,1... | collective-permute-start | bytes 196616 | tf_op jit(solution)/shard_map/ppermute | solution.py:17
  298.6 17.6 %collective-permute-start.13 = (bf16[1,128,256]{2,1,0:T(8,128)(2,1)S(1)}, bf16[1,128,256]{2,1,0:T(8,128)(2,1)S(1)}, u32[]{:S(2)}, u32[]{:S(2)}) collective-permute-start(bf16[1,128,256]{2,1,0:T(8,128)(2,1)S(1)} %get-tuple-element.8), channel_id=1, source_target_pairs={{16,0},{32,16},{48,32},{64,48},{80,64},{96,80},{112,96},{128,112},... | collective-permute-start | bytes 196616 | tf_op jit(solution)/shard_map/ppermute | solution.py:19
  304.3 11.8 %collective-permute-start.15 = (bf16[1,128,256]{2,1,0:T(8,128)(2,1)S(1)}, bf16[1,128,256]{2,1,0:T(8,128)(2,1)S(1)}, u32[]{:S(2)}, u32[]{:S(2)}) collective-permute-start(bf16[1,128,256]{2,1,0:T(8,128)(2,1)S(1)} %get-tuple-element.9), channel_id=1, source_target_pairs={{1,0},{2,1},{3,2},{4,3},{5,4},{6,5},{7,6},{8,7},{9,8},{10,9},{11,1... | collective-permute-start | bytes 196616 | tf_op jit(solution)/shard_map/ppermute | solution.py:19
  316.1 7.1 %copy-start.3 = (bf16[1024,256]{0,1:T(8,128)(2,1)S(1)}, bf16[1024,256]{0,1:T(8,128)(2,1)}, u32[]{:S(2)}) copy-start(bf16[1024,256]{0,1:T(8,128)(2,1)} %get-tuple-element.22) | copy-start | bytes 1572868
where the time goes:
time: 331 us; the launch traced here: 329 us
  blocking collectives  108 us (33%)
  starting transfers between devices  79.1 us (24%)
  waiting for transfers between devices  43.4 us (13%)
  local copies, waits for them, and re-layouts  39.1 us (12%)
  matrix products  31.1 us (9%)
  other arithmetic  27 us (8%)
    all_to_all x2, blocking collectives, sent_to_all(): lax.all_to_all(jnp.broadcast_to(x[None], (size, *x.shape)), axis, 0, 0, t...  67.5 us
    ppermute x8, starting transfers between devices, padded(): lax.ppermute(head, axis, [((i + 1) % count, i) for i in range(ends)])  55.3 us
    all_to_all x1, blocking collectives, sum_at_owner(): lax.all_to_all(pieces, axis, split_axis=0, concat_axis=0, tiled=True)  40.9 us
    all_to_all x1, waiting for transfers between devices, sum_at_owner(): lax.all_to_all(pieces, axis, split_axis=0, concat_axis=0, tiled=True)  37.1 us
    scatter-add x4, other arithmetic, apply_operator(): jnp.zeros(vector.shape, jnp.float32).at[flat_rows].add(coupling_terms)  18.5 us
    ppermute x8, starting transfers between devices, padded(): lax.ppermute(tail, axis, [(i, (i + 1) % count) for i in range(ends)])  17.2 us
    gather x4, local copies, waits for them, and re-layouts, neighbour_faces(): face_vals = vector_b[face_index]  12 us
    dot_general x2, matrix products, per_device(): jnp.dot(local_inv, residual.astype(jnp.bfloat16), preferred_element_type=...  11.8 us
  transfers between devices with their start and end apart: 17, of which 4 were waited for; matrix products, arithmetic and copies ran while one was open for 1% of the time, Pallas kernels for 0%

commit v1 on v0

v1 whole, which is shorter than its diff:
```python
import jax
import jax.numpy as jnp
from jax import lax
from jax.experimental import pallas as pl
from jax.experimental.pallas import tpu as pltpu
from jax.sharding import PartitionSpec as P

STEPS = 2
NLOC = 1024
CPD = 96
NRHS = 256
OVL = 128
COARSE_BLOCK = 1536
GROUP = 384
FACES = 4 * OVL
MESH = pl.DeviceIdType.MESH
F32 = jnp.float32
BF16 = jnp.bfloat16


def dot(a, b):
    return jnp.dot(a, b, preferred_element_type=F32)


def dot_lhs_t(a, b):
    return lax.dot_general(a, b, (((0,), (0,)), ((), ())), preferred_element_type=F32)


def rows(start, size):
    return pl.ds(pl.multiple_of(start, 32), size)


def kernel(
    rhs_h, lmat_h, linv_h, basis_h, cinv_h, couple_h, margin_h,
    sol_out, res_out,
    rhs, lmat, linv, basis, cinv, couple, margin,
    sol, base, base_b, vb, face, face_b, recv,
    gath, acc, part, ybuf, qbuf, zbuf,
    st, wrow, bs, sbt, bt, lsw, sl, slsw, pre, pre_face, coarse_b,
    ag_s, ag_r, rs_s, rs_r, h_s, h_r, ld, out_sem,
):
    r = lax.axis_index("row")
    c = lax.axis_index("col")
    zl, y = r // 4, r % 4
    x, zh, k = c // 4, (c // 2) % 2, c % 2

    loads = [
        pltpu.make_async_copy(s, d, ld.at[i])
        for i, (s, d) in enumerate(
            (
                (rhs_h, rhs), (basis_h, basis), (couple_h, couple), (margin_h, margin),
                (linv_h, linv), (cinv_h, cinv), (lmat_h, lmat),
            )
        )
    ]
    for cp in loads:
        cp.start()

    sibling = (r, x * 4 + zh * 2 + (1 - k))
    z_partner = (r, x * 4 + (1 - zh) * 2 + k)
    shifts = (2, 1, 3)
    x_to = [(r, ((x + d) % 4) * 4 + zh * 2 + k) for d in shifts]
    x_from = [(x + 4 - d) % 4 for d in shifts]
    y_to = [(zl * 4 + (y + d) % 4, c) for d in shifts]
    z_to = [((zl + d) % 4 * 4 + y, c) for d in shifts]
    halo = (
        (r > 0, (r - 1, c), 1),
        (r < 15, (r + 1, c), 0),
        (c > 0, (r, c - 1), 3),
        (c < 15, (r, c + 1), 2),
    )

    for f, (there, _, _2) in enumerate(halo):
        @pl.when(jnp.logical_not(there))
        def _():
            for h in range(2 * STEPS):
                recv[h, pl.ds(f * OVL, OVL), :] = jnp.zeros((OVL, NRHS), BF16)

    barrier = pltpu.get_barrier_semaphore()
    others = [sibling, z_partner] + x_to + y_to + z_to
    for dev in others:
        pl.semaphore_signal(barrier, inc=1, device_id=dev, device_id_type=MESH)
    count = len(others)
    for there, dev, _ in halo:
        @pl.when(there)
        def _():
            pl.semaphore_signal(barrier, inc=1, device_id=dev, device_id_type=MESH)
        count = count + jnp.where(there, 1, 0)

    sends = []

    def send(src, dst, ssem, rsem, dev):
        cp = pltpu.make_async_remote_copy(
            src_ref=src, dst_ref=dst, send_sem=ssem, recv_sem=rsem,
            device_id=dev, device_id_type=MESH,
        )
        cp.start()
        sends.append(cp)
        return cp

    def halo_copy(h, f):
        there, dev, slot = halo[f]
        return pltpu.make_async_remote_copy(
            src_ref=face_b.at[h, pl.ds(f * OVL, OVL)],
            dst_ref=recv.at[h, pl.ds(slot * OVL, OVL)],
            send_sem=h_s.at[h, f], recv_sem=h_r.at[h, slot],
            device_id=dev, device_id_type=MESH,
        )

    def arriving_copy(h, f):
        _, dev, _2 = halo[f]
        return pltpu.make_async_remote_copy(
            src_ref=face_b.at[h, pl.ds(f * OVL, OVL)],
            dst_ref=recv.at[h, pl.ds(f * OVL, OVL)],
            send_sem=h_s.at[h, f], recv_sem=h_r.at[h, f],
            device_id=dev, device_id_type=MESH,
        )

    def halo_start(h):
        for f in (2, 3, 0, 1):
            @pl.when(halo[f][0])
            def _():
                halo_copy(h, f).start()

    def halo_wait(h):
        for f in range(4):
            @pl.when(halo[f][0])
            def _():
                arriving_copy(h, f).wait_recv()

    def halo_sent():
        for h in range(2 * STEPS):
            for f in range(4):
                @pl.when(halo[f][0])
                def _():
                    halo_copy(h, f).wait_send()

    def block(ref, at):
        return ref.at[rows(at * CPD, CPD)]

    def coarse(s, between):
        g = gath.at[s]
        copies = {}

        def go(n, at, dev):
            copies[n] = send(block(g, at), block(g, at), ag_s.at[s, n], ag_r.at[s, n], dev)

        go(0, c, z_partner)
        for j in range(3):
            go(1 + j, c, x_to[j])
        go(4, c, sibling)
        between()
        for j in (1, 2, 0):
            copies[1 + j].wait_recv()
            go(5 + j, x_from[j] * 4 + zh * 2 + k, sibling)
        copies[0].wait_recv()
        zs = x * 4 + (1 - zh) * 2 + k
        for j in range(3):
            go(8 + j, zs, x_to[j])
        go(11, zs, sibling)

        def chunk(xg, first):
            cols = pl.ds(pl.multiple_of(xg * GROUP, 128), GROUP)
            right = g[rows(xg * GROUP, GROUP), :]

            @pl.loop(0, 4)
            def _(m):
                at = rows(m * GROUP, GROUP)
                p = dot(cinv[at, cols], right)
                if first:
                    acc[at, :] = p
                else:
                    acc[at, :] += p

        copies[4].wait_recv()
        copies[11].wait_recv()
        chunk(x, True)
        for j in (1, 2, 0):
            copies[8 + j].wait_recv()
            go(12 + j, x_from[j] * 4 + (1 - zh) * 2 + k, sibling)
        for j in (1, 2):
            copies[5 + j].wait_recv()
            copies[12 + j].wait_recv()
            chunk(x_from[j], False)
        copies[5].wait_recv()
        copies[12].wait_recv()

        p_ref = part.at[s]
        cols = pl.ds(pl.multiple_of(x_from[0] * GROUP, 128), GROUP)
        right = g[rows(x_from[0] * GROUP, GROUP), :]
        ycopies = {}
        for a, dz in enumerate((2, 1, 3, 0)):
            t = (zl + dz) % 4
            at = rows(t * GROUP, GROUP)
            total = acc[at, :] + dot(cinv[at, cols], right)
            acc[at, :] = total
            p_ref[at, :] = total.astype(BF16)
            for j, d in enumerate(shifts):
                n = a * 3 + j
                ycopies[a, j] = send(
                    block(p_ref, t * 4 + (y + d) % 4), ybuf.at[s, n],
                    rs_s.at[s, n], rs_r.at[s, n], y_to[j],
                )
        zcopies = []

        def over_y(a, t):
            for j in range(3):
                ycopies[a, j].wait_recv()
            total = acc[rows((t * 4 + y) * CPD, CPD), :]
            for j in range(3):
                total = total + ybuf[s, a * 3 + j].astype(F32)
            return total

        for a, dz in enumerate((2, 1, 3)):
            t = (zl + dz) % 4
            qbuf[s, a] = over_y(a, t).astype(BF16)
            zcopies.append(
                send(qbuf.at[s, a], zbuf.at[s, a], rs_s.at[s, 12 + a], rs_r.at[s, 12 + a], z_to[a])
            )
        total = over_y(3, zl)
        for a in range(3):
            zcopies[a].wait_recv()
            total = total + zbuf[s, a].astype(F32)
        coarse_b[...] = total.astype(BF16)

    def prepare():
        for i in (2, 3, 4):
            loads[i].wait()
        w = [couple[0, f : f + 1, :] for f in range(4)]

        @pl.loop(0, 8)
        def _(m):
            at = rows(m * 128, 128)
            ids = lax.broadcasted_iota(jnp.int32, (128, OVL), 0) + m * 128
            total = jnp.zeros((128, OVL), F32)
            for f in range(4):
                hit = ids == margin[0, f : f + 1, :]
                st[at, pl.ds(f * OVL, OVL)] = jnp.where(hit, 1.0, 0.0).astype(BF16)
                total = total + jnp.where(hit, w[f], 0.0)
            wrow[at, :] = jnp.broadcast_to(jnp.sum(total, axis=1, keepdims=True), (128, OVL))

        wide = jnp.concatenate(w, axis=1)
        picked = dot(basis[...], st[...])
        bs[...] = (picked * wide).astype(BF16)
        sbt[...] = picked.T.astype(BF16)
        bt[...] = basis[...].astype(F32).T.astype(BF16)

        @pl.loop(0, 4)
        def _(m):
            at = rows(m * 256, 256)
            lsw[at, :] = (dot(linv[at, :], st[...]) * wide).astype(BF16)

        for m in range(4):
            pick = st[:, m * OVL : (m + 1) * OVL].astype(F32).T.astype(BF16)
            at = pl.ds(m * OVL, OVL)
            sl[at, :] = dot(pick, linv[...]).astype(BF16)
            slsw[at, :] = dot(pick, lsw[...]).astype(BF16)
        loads[5].wait()

    def tiles(fn, size=256, total=NLOC):
        @pl.loop(0, total // size)
        def _(m):
            fn(rows(m * size, size))

    loads[0].wait()
    loads[1].wait()
    base_b[...] = rhs[...].astype(BF16)
    gath[0, rows(c * CPD, CPD), :] = dot(basis[...], base_b[...]).astype(BF16)
    pl.semaphore_wait(barrier, count)

    for s in range(STEPS):
        h = 2 * s
        coarse(s, prepare if s == 0 else lambda: None)

        moved = dot(sbt[...], coarse_b[...])
        if s > 0:
            moved = moved + face[...]
        face[...] = moved
        face_b[h] = moved.astype(BF16)
        halo_start(h)

        def correct(at):
            v = dot(bt[at, :], coarse_b[...])
            if s > 0:
                v = v + sol[at, :]
            sol[at, :] = v
            vb[at, :] = v.astype(BF16)

        tiles(correct)
        if s == 0:
            loads[6].wait()

        def defect(at):
            base_b[at, :] = (rhs[at, :] - dot(lmat[at, :], vb[...])).astype(BF16)

        tiles(defect)

        def face_pre(at):
            pre_face[at, :] = face[at, :] + dot(sl[at, :], base_b[...])

        tiles(face_pre, 256, FACES)

        def solve_pre(at):
            sol[at, :] += dot(linv[at, :], base_b[...])

        tiles(solve_pre)
        halo_wait(h)

        moved = pre_face[...] + dot(slsw[...], recv[h])
        face[...] = moved
        face_b[h + 1] = moved.astype(BF16)
        halo_start(h + 1)

        def solve(at):
            v = sol[at, :] + dot(lsw[at, :], recv[h])
            sol[at, :] = v
            vb[at, :] = v.astype(BF16)

        tiles(solve)
        last = s == STEPS - 1
        if last:
            written = pltpu.make_async_copy(sol, sol_out, out_sem.at[0])
            written.start()

        def defect2(at):
            v = rhs[at, :] - dot(lmat[at, :], vb[...])
            if last:
                base[at, :] = v
            else:
                base_b[at, :] = v.astype(BF16)

        tiles(defect2)
        if not last:
            pre[...] = dot(basis[...], base_b[...])
            halo_wait(h + 1)
            gath[s + 1, rows(c * CPD, CPD), :] = (pre[...] + dot(bs[...], recv[h + 1])).astype(BF16)
        else:
            halo_wait(h + 1)

            def finish(at):
                w = jnp.concatenate([wrow[at, :]] * 2, axis=1)
                base[at, :] += w * dot(st[at, :], recv[h + 1])

            tiles(finish)
            residual = pltpu.make_async_copy(base, res_out, out_sem.at[1])
            residual.start()
            written.wait()
            residual.wait()

    for cp in sends:
        cp.wait_send()
    halo_sent()


def per_device(*args):
    any_space = pl.BlockSpec(memory_space=pl.ANY)
    vm = pltpu.VMEM
    dma = pltpu.SemaphoreType.DMA
    scratch = [vm(a.shape, a.dtype) for a in args] + [
        vm((NLOC, NRHS), F32),
        vm((NLOC, NRHS), F32),
        vm((NLOC, NRHS), BF16),
        vm((NLOC, NRHS), BF16),
        vm((FACES, NRHS), F32),
        vm((2 * STEPS, FACES, NRHS), BF16),
        vm((2 * STEPS, FACES, NRHS), BF16),
        vm((STEPS, COARSE_BLOCK, NRHS), BF16),
        vm((COARSE_BLOCK, NRHS), F32),
        vm((STEPS, COARSE_BLOCK, NRHS), BF16),
        vm((STEPS, 12, CPD, NRHS), BF16),
        vm((STEPS, 3, CPD, NRHS), BF16),
        vm((STEPS, 3, CPD, NRHS), BF16),
        vm((NLOC, FACES), BF16),
        vm((NLOC, OVL), F32),
        vm((CPD, FACES), BF16),
        vm((FACES, CPD), BF16),
        vm((NLOC, CPD), BF16),
        vm((NLOC, FACES), BF16),
        vm((FACES, NLOC), BF16),
        vm((FACES, FACES), BF16),
        vm((CPD, NRHS), F32),
        vm((FACES, NRHS), F32),
        vm((CPD, NRHS), BF16),
        dma((STEPS, 15)), dma((STEPS, 15)),
        dma((STEPS, 15)), dma((STEPS, 15)),
        dma((2 * STEPS, 4)), dma((2 * STEPS, 4)),
        dma((len(args),)), dma((2,)),
    ]
    out = jax.ShapeDtypeStruct((NLOC, NRHS), F32)
    return pl.pallas_call(
        kernel,
        out_shape=(out, out),
        in_specs=[any_space] * len(args),
        out_specs=(any_space, any_space),
        scratch_shapes=scratch,
        name="schwarz",
        compiler_params=pltpu.CompilerParams(
            collective_id=0, has_side_effects=True, vmem_limit_bytes=48 << 20
        ),
    )(*args)


def solution(mesh):
    whole = P(("row", "col"), None)
    stacked = P(("row", "col"), None, None)
    return jax.shard_map(
        per_device,
        mesh=mesh,
        in_specs=(whole, whole, whole, whole, P("col", "row"), stacked, stacked),
        out_specs=(whole, whole),
        check_vma=False,
    )
```

time: 331 us -> 97 us (0.29)
  blocking collectives: 108 us -> 0 us
  Pallas kernels: 0 us -> 89.1 us
  starting transfers between devices: 79.1 us -> 0 us
  waiting for transfers between devices: 43.4 us -> 0 us
  local copies, waits for them, and re-layouts: 39.1 us -> 7.04 us
  matrix products: 31.1 us -> 0 us
  other arithmetic: 27 us -> 0 us
    all_to_all x3 -> x0, blocking collectives: 108 us -> none  [the longest x2 67.5 us: sent_to_all(): lax.all_to_all(jnp.broadcast_to(x[None], (size, *x.shape)), axis, 0, 0, t...]
    pallas_call x0 -> x1, Pallas kernels: none -> 89.1 us  [per_device(): pl.pallas_call(kernel, out_shape=(out, out), in_specs=[any_space] * len(a...]
    ppermute x16 -> x0, starting transfers between devices: 72.5 us -> none  [the longest x8 55.3 us: padded(): lax.ppermute(head, axis, [((i + 1) % count, i) for i in range(ends)])]
    all_to_all x1 -> x0, waiting for transfers between devices: 37.1 us -> none  [sum_at_owner(): lax.all_to_all(pieces, axis, split_axis=0, concat_axis=0, tiled=True)]
    dot_general x9 -> x0, matrix products: 31.1 us -> none  [the longest x2 11.8 us: per_device(): jnp.dot(local_inv, residual.astype(jnp.bfloat16), preferred_element_type=...]
    scatter-add x4 -> x0, other arithmetic: 18.5 us -> none  [apply_operator(): jnp.zeros(vector.shape, jnp.float32).at[flat_rows].add(coupling_terms)]
    gather x4 -> x0, local copies, waits for them, and re-layouts: 12 us -> none  [neighbour_faces(): face_vals = vector_b[face_index]]
    convert_element_type x4 -> x0, local copies, waits for them, and re-layouts: 8.18 us -> none  [apply_operator(): vector_b = vector.astype(jnp.bfloat16)]
  transfers between devices with their start and end apart: 17 -> 0, of which waited for: 4 -> 0; matrix products, arithmetic and copies ran while one was open for 1% -> 0% of each run, Pallas kernels for 0% -> 0%
where the time goes in v1:
time: 97 us; the launch traced here: 96.8 us
  Pallas kernels  89.1 us (92%)
  local copies, waits for them, and re-layouts  7.04 us (7%)
    pallas_call x1, Pallas kernels, per_device(): pl.pallas_call(kernel, out_shape=(out, out), in_specs=[any_space] * len(a...  89.1 us
    unnamed x12, local copies, waits for them, and re-layouts  7.04 us

profile of v1, /device:TPU:34, one launch (start us, length us, event | category | flops | bytes accessed | tf_op | source)
XLA Modules:
  0.0 96.8 jit_solution(18410055954858900536)
XLA Ops:
  0.6 0.0 copy-start
  0.6 1.6 %copy-done = bf16[1024,1024]{1,0:T(8,128)(2,1)S(1)} copy-done((bf16[1024,1024]{1,0:T(8,128)(2,1)S(1)}, bf16[1024,1024]{1,0:T(8,128)(2,1)}, u32[]{:S(2)}) %copy-start) | copy-done | bytes 2097176
  2.2 0.0 copy-start.1
  2.2 1.2 %copy-done.1 = f32[1024,256]{1,0:T(8,128)S(1)} copy-done((f32[1024,256]{1,0:T(8,128)S(1)}, f32[1024,256]{1,0:T(8,128)}, u32[]{:S(2)}) %copy-start.1) | copy-done | bytes 1048600
  3.4 0.0 copy-start.2
  3.5 0.9 copy-done.2
  4.4 0.0 copy-start.3
  4.4 0.7 copy-done.3
  5.1 0.0 copy-start.4
  5.1 0.7 copy-done.4
  5.7 89.1 %schwarz.1 = (f32[1024,256]{1,0:T(8,128)S(1)}, f32[1024,256]{1,0:T(8,128)S(1)}) custom-call(f32[1024,256]{1,0:T(8,128)S(1)} %copy-done.1, bf16[1024,1024]{1,0:T(8,128)(2,1)S(1)} %copy-done, bf16[1024,1024]{1,0:T(8,128)(2,1)} %linv_h.1, bf16[96,1024]{1,0:T(8,128)(2,1)S(1)} %copy-done.2, bf16[1536,1536]{1,0:T(8,128)(2,1)} %cinv_h.1, ...), custom_call_target="tpu_custom_call" | custom-call | tf_op jit(solution)/shard_map/schwarz/pallas_call | solution.py:390
  94.8 1.0 %copy.11 = f32[1024,256]{1,0:T(8,128)} copy(f32[1024,256]{1,0:T(8,128)S(1)} %get-tuple-element.4) | data formatting | bytes 2097152
  95.8 1.0 %copy.12 = f32[1024,256]{1,0:T(8,128)} copy(f32[1024,256]{1,0:T(8,128)S(1)} %get-tuple-element.5) | data formatting | bytes 2097152
Async XLA Ops:
  0.6 1.6 %copy-start = (bf16[1024,1024]{1,0:T(8,128)(2,1)S(1)}, bf16[1024,1024]{1,0:T(8,128)(2,1)}, u32[]{:S(2)}) copy-start(bf16[1024,1024]{1,0:T(8,128)(2,1)} %lmat_h.1) | copy-start | bytes 6291460
  2.2 1.2 %copy-start.1 = (f32[1024,256]{1,0:T(8,128)S(1)}, f32[1024,256]{1,0:T(8,128)}, u32[]{:S(2)}) copy-start(f32[1024,256]{1,0:T(8,128)} %rhs_h.1) | copy-start | bytes 3145732
  3.4 0.9 copy-start.2
  4.4 0.7 copy-start.3
  5.1 0.7 copy-start.4

commit v2 on v1

v2 whole, which is shorter than its diff:
```python
import jax
import jax.numpy as jnp
from jax import lax
from jax.experimental import pallas as pl
from jax.experimental.pallas import tpu as pltpu
from jax.sharding import PartitionSpec as P

STEPS = 2
NLOC = 1024
CPD = 96
NRHS = 256
OVL = 128
COARSE_BLOCK = 1536
GROUP = 384
FACES = 4 * OVL
PARTS = 2
WIDTH = NRHS // PARTS
MESH = pl.DeviceIdType.MESH
F32 = jnp.float32
BF16 = jnp.bfloat16


def dot(a, b):
    return jnp.dot(a, b, preferred_element_type=F32)


def dot_lhs_t(a, b):
    return lax.dot_general(a, b, (((0,), (0,)), ((), ())), preferred_element_type=F32)


def rows(start, size):
    return pl.ds(pl.multiple_of(start, 32), size)


def kernel(
    rhs_h, lmat_h, linv_h, basis_h, cinv_h, couple_h, margin_h,
    sol_out, base_out, recv_out, st_out, wrow_out,
    rhs, lmat, linv, basis, cinv, couple, margin,
    sol, base, base_b, vb, face, face_b, recv,
    gath, acc, part, ybuf, qbuf, zbuf,
    st, wrow, bs, sbt, bt, lsw, sl, slsw, pre, pre_face, coarse_b,
    ag_s, ag_r, rs_s, rs_r, h_s, h_r, ld, out_sem,
):
    r = lax.axis_index("row")
    c = lax.axis_index("col")
    zl, y = r // 4, r % 4
    x, zh, k = c // 4, (c // 2) % 2, c % 2

    loads = [
        pltpu.make_async_copy(s, d, ld.at[i])
        for i, (s, d) in enumerate(
            (
                (rhs_h, rhs), (basis_h, basis), (couple_h, couple), (margin_h, margin),
                (linv_h, linv), (cinv_h, cinv), (lmat_h, lmat),
            )
        )
    ]
    for cp in loads[:4]:
        cp.start()

    sibling = (r, x * 4 + zh * 2 + (1 - k))
    z_partner = (r, x * 4 + (1 - zh) * 2 + k)
    shifts = (2, 1, 3)
    x_to = [(r, ((x + d) % 4) * 4 + zh * 2 + k) for d in shifts]
    x_from = [(x + 4 - d) % 4 for d in shifts]
    y_to = [(zl * 4 + (y + d) % 4, c) for d in shifts]
    z_other = [3 - 3 * (zl // 2), 2 - zl // 2, zl + 1 - 2 * (zl % 2)]
    z_to = [(t * 4 + y, c) for t in z_other]
    halo = (
        (r > 0, (r - 1, c), 1),
        (r < 15, (r + 1, c), 0),
        (c > 0, (r, c - 1), 3),
        (c < 15, (r, c + 1), 2),
    )

    for f, (there, _, _2) in enumerate(halo):
        @pl.when(jnp.logical_not(there))
        def _():
            for h in range(2 * STEPS):
                for p in range(PARTS):
                    recv[h, p, pl.ds(f * OVL, OVL), :] = jnp.zeros((OVL, WIDTH), BF16)

    barrier = pltpu.get_barrier_semaphore()
    others = [sibling, z_partner] + x_to + y_to + z_to
    for dev in others:
        pl.semaphore_signal(barrier, inc=1, device_id=dev, device_id_type=MESH)
    count = len(others)
    for there, dev, _ in halo:
        @pl.when(there)
        def _():
            pl.semaphore_signal(barrier, inc=1, device_id=dev, device_id_type=MESH)
        count = count + jnp.where(there, 1, 0)

    sends = []

    def send(src, dst, ssem, rsem, dev):
        cp = pltpu.make_async_remote_copy(
            src_ref=src, dst_ref=dst, send_sem=ssem, recv_sem=rsem,
            device_id=dev, device_id_type=MESH,
        )
        cp.start()
        sends.append(cp)
        return cp

    def lanes(p):
        return pl.ds(p * WIDTH, WIDTH)

    def halo_copy(h, p, f, slot):
        return pltpu.make_async_remote_copy(
            src_ref=face_b.at[h, p, pl.ds(f * OVL, OVL)],
            dst_ref=recv.at[h, p, pl.ds(slot * OVL, OVL)],
            send_sem=h_s.at[h, p, f], recv_sem=h_r.at[h, p, slot],
            device_id=halo[f][1], device_id_type=MESH,
        )

    def halo_start(h, p):
        for f in (2, 3, 0, 1):
            @pl.when(halo[f][0])
            def _():
                halo_copy(h, p, f, halo[f][2]).start()

    def halo_wait(h, p):
        for f in (1, 0, 3, 2):
            @pl.when(halo[f][0])
            def _():
                halo_copy(h, p, f, f).wait_recv()

    def halo_sent():
        for h in range(2 * STEPS):
            for p in range(PARTS):
                for f in range(4):
                    @pl.when(halo[f][0])
                    def _():
                        halo_copy(h, p, f, halo[f][2]).wait_send()

    def block(ref, at):
        return ref.at[rows(at * CPD, CPD)]

    copies = {}
    own = [xg * 4 + zh * 2 + k for xg in x_from]
    other = [xg * 4 + (1 - zh) * 2 + k for xg in x_from]
    across = x * 4 + (1 - zh) * 2 + k

    def go(s, p, n, at, dev):
        g = gath.at[s, p]
        copies[p, n] = send(block(g, at), block(g, at), ag_s.at[s, p, n], ag_r.at[s, p, n], dev)

    def gather_start(s, p):
        go(s, p, 0, c, z_partner)
        for j in range(3):
            go(s, p, 1 + j, c, x_to[j])
        go(s, p, 4, c, sibling)

    def chunk(s, p, xg, first):
        cols = pl.ds(pl.multiple_of(xg * GROUP, 128), GROUP)
        right = gath[s, p, rows(xg * GROUP, GROUP), :]
        for m in range(4):
            at = pl.ds(m * GROUP, GROUP)
            v = dot(cinv[at, cols], right)
            if first:
                acc[p, at, :] = v
            else:
                acc[p, at, :] += v

    def coarse(s, before, after):
        before()
        for p in range(PARTS):
            for j in (1, 2, 0):
                copies[p, 1 + j].wait_recv()
                go(s, p, 5 + j, own[j], sibling)
        for p in range(PARTS):
            copies[p, 0].wait_recv()
            for j in range(3):
                go(s, p, 8 + j, across, x_to[j])
            go(s, p, 11, across, sibling)
        for p in range(PARTS):
            copies[p, 4].wait_recv()
            copies[p, 11].wait_recv()
            chunk(s, p, x, True)
        for p in range(PARTS):
            for j in (1, 2, 0):
                copies[p, 8 + j].wait_recv()
                go(s, p, 12 + j, other[j], sibling)
        ycopies = {}
        for p in range(PARTS):
            for j in (1, 2):
                copies[p, 5 + j].wait_recv()
                copies[p, 12 + j].wait_recv()
                chunk(s, p, x_from[j], False)
            copies[p, 5].wait_recv()
            copies[p, 12].wait_recv()

            p_ref = part.at[s, p]
            cols = pl.ds(pl.multiple_of(x_from[0] * GROUP, 128), GROUP)
            right = gath[s, p, rows(x_from[0] * GROUP, GROUP), :]
            for a, t in enumerate(z_other + [zl]):
                at = rows(t * GROUP, GROUP)
                total = acc[p, at, :] + dot(cinv[at, cols], right)
                acc[p, at, :] = total
                p_ref[at, :] = total.astype(BF16)
                for j, d in enumerate(shifts):
                    n = a * 3 + j
                    ycopies[p, a, j] = send(
                        block(p_ref, t * 4 + (y + d) % 4), ybuf.at[s, p, n],
                        rs_s.at[s, p, n], rs_r.at[s, p, n], y_to[j],
                    )
        after()

        def over_y(p, a, t):
            for j in range(3):
                ycopies[p, a, j].wait_recv()
            total = acc[p, rows((t * 4 + y) * CPD, CPD), :]
            for j in range(3):
                total = total + ybuf[s, p, a * 3 + j].astype(F32)
            return total

        for p in range(PARTS):
            for a, t in enumerate(z_other):
                qbuf[s, p, a] = over_y(p, a, t).astype(BF16)
                send(
                    qbuf.at[s, p, a], zbuf.at[s, p, zl],
                    rs_s.at[s, p, 12 + a], rs_r.at[s, p, 12 + zl], z_to[a],
                )
        for p in range(PARTS):
            total = over_y(p, 3, zl)
            for a, t in reversed(list(enumerate(z_other))):
                pltpu.make_async_remote_copy(
                    src_ref=qbuf.at[s, p, a], dst_ref=zbuf.at[s, p, t],
                    send_sem=rs_s.at[s, p, 12 + a], recv_sem=rs_r.at[s, p, 12 + t],
                    device_id=z_to[a], device_id_type=MESH,
                ).wait_recv()
                total = total + zbuf[s, p, t].astype(F32)
            coarse_b[:, lanes(p)] = total.astype(BF16)
            moved = dot(sbt[...], coarse_b[:, lanes(p)])
            if s > 0:
                moved = moved + face[:, lanes(p)]
            face[:, lanes(p)] = moved
            face_b[2 * s, p] = moved.astype(BF16)
            halo_start(2 * s, p)

    def prepare_faces():
        for i in (2, 3):
            loads[i].wait()
        w = [couple[0, f : f + 1, :] for f in range(4)]
        for m in range(4):
            at = pl.ds(m * 256, 256)
            ids = lax.broadcasted_iota(jnp.int32, (256, OVL), 0) + m * 256
            total = jnp.zeros((256, OVL), F32)
            for f in range(4):
                hit = ids == margin[0, f : f + 1, :]
                st[at, pl.ds(f * OVL, OVL)] = jnp.where(hit, 1.0, 0.0).astype(BF16)
                total = total + jnp.where(hit, w[f], 0.0)
            wrow[at, :] = jnp.broadcast_to(jnp.sum(total, axis=1, keepdims=True), (256, OVL))
        keep(4, st, st_out)
        keep(5, wrow, wrow_out)
        loads[5].wait()

    def prepare_local():
        loads[4].wait()
        wide = jnp.concatenate([couple[0, f : f + 1, :] for f in range(4)], axis=1)
        picked = dot(basis[...], st[...])
        bs[...] = (picked * wide).astype(BF16)
        sbt[...] = picked.T.astype(BF16)
        bt[...] = basis[...].astype(F32).T.astype(BF16)
        for m in range(4):
            at = pl.ds(m * 256, 256)
            lsw[at, :] = (dot(linv[at, :], st[...]) * wide).astype(BF16)
        for m in range(4):
            pick = st[:, m * OVL : (m + 1) * OVL].astype(F32).T.astype(BF16)
            at = pl.ds(m * OVL, OVL)
            sl[at, :] = dot(pick, linv[...]).astype(BF16)
            slsw[at, :] = dot(pick, lsw[...]).astype(BF16)

    def tiles(fn, size=256, total=NLOC):
        for m in range(total // size):
            fn(pl.ds(m * size, size))

    kept = []

    def keep(n, src, dst):
        cp = pltpu.make_async_copy(src, dst, out_sem.at[n])
        cp.start()
        kept.append(cp)

    loads[0].wait()
    base_b[...] = rhs[...].astype(BF16)
    loads[1].wait()
    first = dot(basis[...], base_b[...]).astype(BF16)
    for p in range(PARTS):
        gath[0, p, rows(c * CPD, CPD), :] = first[:, p * WIDTH : (p + 1) * WIDTH]
    for cp in loads[4:]:
        cp.start()
    pl.semaphore_wait(barrier, count)
    for p in range(PARTS):
        gather_start(0, p)

    for s in range(STEPS):
        h = 2 * s
        last = s == STEPS - 1
        coarse(s, *((prepare_faces, prepare_local) if s == 0 else (lambda: None,) * 2))

        def correct(at):
            v = dot(bt[at, :], coarse_b[...])
            if s > 0:
                v = v + sol[at, :]
            sol[at, :] = v
            vb[at, :] = v.astype(BF16)

        tiles(correct)
        if s == 0:
            loads[6].wait()

        def defect(at):
            base_b[at, :] = (rhs[at, :] - dot(lmat[at, :], vb[...])).astype(BF16)

        tiles(defect)

        def face_pre(at):
            pre_face[at, :] = face[at, :] + dot(sl[at, :], base_b[...])

        tiles(face_pre, 256, FACES)

        for p in range(PARTS):
            halo_wait(h, p)
            moved = pre_face[:, lanes(p)] + dot(slsw[...], recv[h, p])
            face[:, lanes(p)] = moved
            face_b[h + 1, p] = moved.astype(BF16)
            halo_start(h + 1, p)

        def solve(at):
            v = sol[at, :] + dot(linv[at, :], base_b[...])
            for p in range(PARTS):
                w = v[:, p * WIDTH : (p + 1) * WIDTH] + dot(lsw[at, :], recv[h, p])
                sol[at, lanes(p)] = w
                vb[at, lanes(p)] = w.astype(BF16)

        tiles(solve)
        if last:
            keep(0, sol, sol_out)

        def defect2(at):
            v = rhs[at, :] - dot(lmat[at, :], vb[...])
            if last:
                base[at, :] = v
            else:
                base_b[at, :] = v.astype(BF16)

        tiles(defect2)
        if not last:
            pre[...] = dot(basis[...], base_b[...])
            for p in range(PARTS):
                halo_wait(h + 1, p)
                gath[s + 1, p, rows(c * CPD, CPD), :] = (
                    pre[:, lanes(p)] + dot(bs[...], recv[h + 1, p])
                ).astype(BF16)
                gather_start(s + 1, p)
        else:
            keep(1, base, base_out)
            for p in range(PARTS):
                halo_wait(h + 1, p)
                keep(2 + p, recv.at[h + 1, p], recv_out.at[p])

    for cp in kept:
        cp.wait()
    for cp in sends:
        cp.wait_send()
    halo_sent()


def last_residual(sol, base, recv, st, wrow, sol_out, res_out, res, sem):
    copies = [pltpu.make_async_copy(sol, sol_out, sem.at[4])]
    copies[0].start()
    right = jnp.concatenate([recv[p] for p in range(PARTS)], axis=1)
    for m in range(4):
        at = pl.ds(m * 256, 256)
        w = jnp.concatenate([wrow[at, :]] * PARTS, axis=1)
        res[at, :] = base[at, :] + w * dot(st[at, :], right)
        cp = pltpu.make_async_copy(res.at[at], res_out.at[at], sem.at[m])
        cp.start()
        copies.append(cp)
    for cp in copies:
        cp.wait()


def per_device(*args):
    args = [pltpu.with_memory_space_constraint(a, pltpu.HBM) for a in args]
    any_space = pl.BlockSpec(memory_space=pl.ANY)
    vm = pltpu.VMEM
    dma = pltpu.SemaphoreType.DMA
    scratch = [vm(a.shape, a.dtype) for a in args] + [
        vm((NLOC, NRHS), F32),
        vm((NLOC, NRHS), F32),
        vm((NLOC, NRHS), BF16),
        vm((NLOC, NRHS), BF16),
        vm((FACES, NRHS), F32),
        vm((2 * STEPS, PARTS, FACES, WIDTH), BF16),
        vm((2 * STEPS, PARTS, FACES, WIDTH), BF16),
        vm((STEPS, PARTS, COARSE_BLOCK, WIDTH), BF16),
        vm((PARTS, COARSE_BLOCK, WIDTH), F32),
        vm((STEPS, PARTS, COARSE_BLOCK, WIDTH), BF16),
        vm((STEPS, PARTS, 12, CPD, WIDTH), BF16),
        vm((STEPS, PARTS, 3, CPD, WIDTH), BF16),
        vm((STEPS, PARTS, 4, CPD, WIDTH), BF16),
        vm((NLOC, FACES), BF16),
        vm((NLOC, OVL), F32),
        vm((CPD, FACES), BF16),
        vm((FACES, CPD), BF16),
        vm((NLOC, CPD), BF16),
        vm((NLOC, FACES), BF16),
        vm((FACES, NLOC), BF16),
        vm((FACES, FACES), BF16),
        vm((CPD, NRHS), F32),
        vm((FACES, NRHS), F32),
        vm((CPD, NRHS), BF16),
        dma((STEPS, PARTS, 15)), dma((STEPS, PARTS, 15)),
        dma((STEPS, PARTS, 15)), dma((STEPS, PARTS, 16)),
        dma((2 * STEPS, PARTS, 4)), dma((2 * STEPS, PARTS, 4)),
        dma((len(args),)), dma((6,)),
    ]
    out = jax.ShapeDtypeStruct((NLOC, NRHS), F32)
    handed_on = (
        out,
        out,
        jax.ShapeDtypeStruct((PARTS, FACES, WIDTH), BF16),
        jax.ShapeDtypeStruct((NLOC, FACES), BF16),
        jax.ShapeDtypeStruct((NLOC, OVL), F32),
    )
    handed = pl.pallas_call(
        kernel,
        out_shape=handed_on,
        in_specs=[any_space] * len(args),
        out_specs=(any_space,) * 5,
        scratch_shapes=scratch,
        name="schwarz",
        compiler_params=pltpu.CompilerParams(
            collective_id=0, has_side_effects=True, vmem_limit_bytes=48 << 20
        ),
    )(*args)
    return pl.pallas_call(
        last_residual,
        out_shape=(out, out),
        in_specs=[any_space] + [pl.BlockSpec(memory_space=vm)] * 4,
        out_specs=(pl.BlockSpec(memory_space=pltpu.HBM), pl.BlockSpec(memory_space=pltpu.HBM)),
        scratch_shapes=[vm((NLOC, NRHS), F32), dma((5,))],
        name="last_residual",
        compiler_params=pltpu.CompilerParams(vmem_limit_bytes=24 << 20),
    )(*handed)


def solution(mesh):
    whole = P(("row", "col"), None)
    stacked = P(("row", "col"), None, None)
    return jax.shard_map(
        per_device,
        mesh=mesh,
        in_specs=(whole, whole, whole, whole, P("col", "row"), stacked, stacked),
        out_specs=(whole, whole),
        check_vma=False,
    )
```

time: 97 us -> 83.3 us (0.86)
  Pallas kernels: 89.1 us -> 81.4 us
  local copies, waits for them, and re-layouts: 7.04 us -> 0 us
    pallas_call x1 -> x2, Pallas kernels: 89.1 us -> 81.4 us  [the longest x1 80 us: per_device(): pl.pallas_call(kernel, out_shape=handed_on, in_specs=[any_space] * len(ar...]
    unnamed x12 -> x0, local copies, waits for them, and re-layouts: 7.04 us -> none
where the time goes in v2:
time: 83.3 us; the launch traced here: 82.2 us
  Pallas kernels  81.4 us (98%)
    pallas_call x1, Pallas kernels, per_device(): pl.pallas_call(kernel, out_shape=handed_on, in_specs=[any_space] * len(ar...  80 us

profile of v2, /device:TPU:34, one launch (start us, length us, event | category | flops | bytes accessed | tf_op | source)
XLA Modules:
  0.0 82.2 jit_solution(6854546995520014908)
XLA Ops:
  0.6 80.0 %schwarz.1 = (f32[1024,256]{1,0:T(8,128)S(1)}, f32[1024,256]{1,0:T(8,128)S(1)}, bf16[2,512,128]{2,1,0:T(8,128)(2,1)S(1)}, bf16[1024,512]{1,0:T(8,128)(2,1)S(1)}, f32[1024,128]{1,0:T(8,128)S(1)}) custom-call(f32[1024,256]{1,0:T(8,128)} %rhs_h.1, bf16[1024,1024]{1,0:T(8,128)(2,1)} %lmat_h.1, bf16[1024,1024]{1,0:T(8,128)(2,1)} %linv_h.1, ...), custom_call_target="tpu_custom_call" | custom-call | tf_op jit(solution)/shard_map/schwarz/pallas_call | solution.py:428
  80.7 1.4 %last_residual.1 = (f32[1024,256]{1,0:T(8,128)}, f32[1024,256]{1,0:T(8,128)}) custom-call(f32[1024,256]{1,0:T(8,128)S(1)} %get-tuple-element.7.sol, f32[1024,256]{1,0:T(8,128)S(1)} %get-tuple-element.8.base, bf16[2,512,128]{2,1,0:T(8,128)(2,1)S(1)} %get-tuple-element.9.recv, bf16[1024,512]{1,0:T(8,128)(2,1)S(1)} %get-tuple-element.10.st, ...), custom_call_target="tpu_custom_call" | custom-call | tf_op jit(solution)/shard_map/last_residual/pallas_call | solution.py:439

commit v3 on v2

--- a/solution.py
+++ b/solution.py
@@ -145,8 +145,10 @@
         g = gath.at[s, p]
         copies[p, n] = send(block(g, at), block(g, at), ag_s.at[s, p, n], ag_r.at[s, p, n], dev)
 
-    def gather_start(s, p):
+    def gather_z(s, p):
         go(s, p, 0, c, z_partner)
+
+    def gather_rest(s, p):
         for j in range(3):
             go(s, p, 1 + j, c, x_to[j])
         go(s, p, 4, c, sibling)
@@ -177,16 +179,37 @@
             copies[p, 4].wait_recv()
             copies[p, 11].wait_recv()
             chunk(s, p, x, True)
-        for p in range(PARTS):
-            for j in (1, 2, 0):
-                copies[p, 8 + j].wait_recv()
-                go(s, p, 12 + j, other[j], sibling)
+        def pass_on(p, j):
+            copies[p, 8 + j].wait_recv()
+            go(s, p, 12 + j, other[j], sibling)
+
+        def early(p, j):
+            copies[p, 5 + j].wait_recv()
+            copies[p, 12 + j].wait_recv()
+            chunk(s, p, x_from[j], False)
+
+        for p in range(PARTS):
+            for j in (1, 2):
+                pass_on(p, j)
+        pass_on(0, 0)
+        early(0, 1)
+        pass_on(1, 0)
+        early(0, 2)
         ycopies = {}
-        for p in range(PARTS):
-            for j in (1, 2):
-                copies[p, 5 + j].wait_recv()
-                copies[p, 12 + j].wait_recv()
-                chunk(s, p, x_from[j], False)
+
+        def over_links(p, a, t):
+            p_ref = part.at[s, p]
+            for j, d in enumerate(shifts):
+                n = a * 3 + j
+                ycopies[p, a, j] = send(
+                    block(p_ref, t * 4 + (y + d) % 4), ybuf.at[s, p, n],
+                    rs_s.at[s, p, n], rs_r.at[s, p, n], y_to[j],
+                )
+
+        for p in range(PARTS):
+            if p > 0:
+                early(p, 1)
+                early(p, 2)
             copies[p, 5].wait_recv()
             copies[p, 12].wait_recv()
 
@@ -198,12 +221,10 @@
                 total = acc[p, at, :] + dot(cinv[at, cols], right)
                 acc[p, at, :] = total
                 p_ref[at, :] = total.astype(BF16)
-                for j, d in enumerate(shifts):
-                    n = a * 3 + j
-                    ycopies[p, a, j] = send(
-                        block(p_ref, t * 4 + (y + d) % 4), ybuf.at[s, p, n],
-                        rs_s.at[s, p, n], rs_r.at[s, p, n], y_to[j],
-                    )
+                if a < 3:
+                    over_links(p, a, t)
+        for p in range(PARTS):
+            over_links(p, 3, zl)
         after()
 
         def over_y(p, a, t):
@@ -292,7 +313,9 @@
         cp.start()
     pl.semaphore_wait(barrier, count)
     for p in range(PARTS):
-        gather_start(0, p)
+        gather_z(0, p)
+    for p in range(PARTS):
+        gather_rest(0, p)
 
     for s in range(STEPS):
         h = 2 * s
@@ -353,7 +376,8 @@
                 gath[s + 1, p, rows(c * CPD, CPD), :] = (
                     pre[:, lanes(p)] + dot(bs[...], recv[h + 1, p])
                 ).astype(BF16)
-                gather_start(s + 1, p)
+                gather_z(s + 1, p)
+                gather_rest(s + 1, p)
         else:
             keep(1, base, base_out)
             for p in range(PARTS):

time: 83.3 us -> 81.2 us (0.975)
  Pallas kernels: 81.4 us -> 79.3 us
    pallas_call x1, Pallas kernels: 80 us -> 78 us  [per_device(): pl.pallas_call(kernel, out_shape=handed_on, in_specs=[any_space] * len(ar...]
where the time goes in v3:
time: 81.2 us; the launch traced here: 80.1 us
  Pallas kernels  79.3 us (98%)
    pallas_call x1, Pallas kernels, per_device(): pl.pallas_call(kernel, out_shape=handed_on, in_specs=[any_space] * len(ar...  78 us

profile of v3, /device:TPU:34, one launch (start us, length us, event | category | flops | bytes accessed | tf_op | source)
XLA Modules:
  0.0 80.1 jit_solution(9474336603574497363)
XLA Ops:
  0.6 78.0 %schwarz.1 = (f32[1024,256]{1,0:T(8,128)S(1)}, f32[1024,256]{1,0:T(8,128)S(1)}, bf16[2,512,128]{2,1,0:T(8,128)(2,1)S(1)}, bf16[1024,512]{1,0:T(8,128)(2,1)S(1)}, f32[1024,128]{1,0:T(8,128)S(1)}) custom-call(f32[1024,256]{1,0:T(8,128)} %rhs_h.1, bf16[1024,1024]{1,0:T(8,128)(2,1)} %lmat_h.1, bf16[1024,1024]{1,0:T(8,128)(2,1)} %linv_h.1, ...), custom_call_target="tpu_custom_call" | custom-call | tf_op jit(solution)/shard_map/schwarz/pallas_call | solution.py:452
  78.6 1.4 %last_residual.1 = (f32[1024,256]{1,0:T(8,128)}, f32[1024,256]{1,0:T(8,128)}) custom-call(f32[1024,256]{1,0:T(8,128)S(1)} %get-tuple-element.7.sol, f32[1024,256]{1,0:T(8,128)S(1)} %get-tuple-element.8.base, bf16[2,512,128]{2,1,0:T(8,128)(2,1)S(1)} %get-tuple-element.9.recv, bf16[1024,512]{1,0:T(8,128)(2,1)S(1)} %get-tuple-element.10.st, ...), custom_call_target="tpu_custom_call" | custom-call | tf_op jit(solution)/shard_map/last_residual/pallas_call | solution.py:463

commit v4 on v3

--- a/solution.py
+++ b/solution.py
@@ -37,7 +37,7 @@
     sol_out, base_out, recv_out, st_out, wrow_out,
     rhs, lmat, linv, basis, cinv, couple, margin,
     sol, base, base_b, vb, face, face_b, recv,
-    gath, acc, part, ybuf, qbuf, zbuf,
+    gath, acc, part, ybuf, qbuf, zbuf, xbuf, xsum, xin,
     st, wrow, bs, sbt, bt, lsw, sl, slsw, pre, pre_face, coarse_b,
     ag_s, ag_r, rs_s, rs_r, h_s, h_r, ld, out_sem,
 ):
@@ -199,7 +199,14 @@
 
         def over_links(p, a, t):
             p_ref = part.at[s, p]
+            if p == 0 and a < 3:
+                send(
+                    block(p_ref, t * 4 + (y + 2) % 4), xbuf.at[s, zl],
+                    rs_s.at[s, p, 15 + a], rs_r.at[s, p, 16 + zl], z_to[a],
+                )
             for j, d in enumerate(shifts):
+                if p == 0 and j == 0:
+                    continue
                 n = a * 3 + j
                 ycopies[p, a, j] = send(
                     block(p_ref, t * 4 + (y + d) % 4), ybuf.at[s, p, n],
@@ -228,29 +235,47 @@
         after()
 
         def over_y(p, a, t):
-            for j in range(3):
+            ways = (1, 2) if p == 0 else (0, 1, 2)
+            for j in ways:
                 ycopies[p, a, j].wait_recv()
             total = acc[p, rows((t * 4 + y) * CPD, CPD), :]
-            for j in range(3):
+            for j in ways:
                 total = total + ybuf[s, p, a * 3 + j].astype(F32)
             return total
 
-        for p in range(PARTS):
-            for a, t in enumerate(z_other):
-                qbuf[s, p, a] = over_y(p, a, t).astype(BF16)
-                send(
-                    qbuf.at[s, p, a], zbuf.at[s, p, zl],
-                    rs_s.at[s, p, 12 + a], rs_r.at[s, p, 12 + zl], z_to[a],
-                )
+        def toward_owner(p, a):
+            qbuf[s, p, a] = over_y(p, a, z_other[a]).astype(BF16)
+            send(
+                qbuf.at[s, p, a], zbuf.at[s, p, zl],
+                rs_s.at[s, p, 12 + a], rs_r.at[s, p, 12 + zl], z_to[a],
+            )
+
+        def arrived(p, a, src, dst, at):
+            t = z_other[a]
+            pltpu.make_async_remote_copy(
+                src_ref=src.at[a], dst_ref=dst.at[t],
+                send_sem=rs_s.at[s, p, 12 + a], recv_sem=rs_r.at[s, p, at + t],
+                device_id=z_to[a], device_id_type=MESH,
+            ).wait_recv()
+            return dst[t].astype(F32)
+
+        for a in range(3):
+            toward_owner(0, a)
+        toward_owner(1, 0)
+        total = acc[0, rows((zl * 4 + (y + 2) % 4) * CPD, CPD), :]
+        for a in range(3):
+            total = total + arrived(0, a, qbuf.at[s, 0], xbuf.at[s], 16)
+        xsum[s] = total.astype(BF16)
+        from_far = send(xsum.at[s], xin.at[s], rs_s.at[s, 0, 18], rs_r.at[s, 0, 20], y_to[0])
+        for a in (1, 2):
+            toward_owner(1, a)
         for p in range(PARTS):
             total = over_y(p, 3, zl)
-            for a, t in reversed(list(enumerate(z_other))):
-                pltpu.make_async_remote_copy(
-                    src_ref=qbuf.at[s, p, a], dst_ref=zbuf.at[s, p, t],
-                    send_sem=rs_s.at[s, p, 12 + a], recv_sem=rs_r.at[s, p, 12 + t],
-                    device_id=z_to[a], device_id_type=MESH,
-                ).wait_recv()
-                total = total + zbuf[s, p, t].astype(F32)
+            for a in (2, 1, 0):
+                total = total + arrived(p, a, qbuf.at[s, p], zbuf.at[s, p], 12)
+            if p == 0:
+                from_far.wait_recv()
+                total = total + xin[s].astype(F32)
             coarse_b[:, lanes(p)] = total.astype(BF16)
             moved = dot(sbt[...], coarse_b[:, lanes(p)])
             if s > 0:
@@ -425,6 +450,9 @@
         vm((STEPS, PARTS, 12, CPD, WIDTH), BF16),
         vm((STEPS, PARTS, 3, CPD, WIDTH), BF16),
         vm((STEPS, PARTS, 4, CPD, WIDTH), BF16),
+        vm((STEPS, 4, CPD, WIDTH), BF16),
+        vm((STEPS, CPD, WIDTH), BF16),
+        vm((STEPS, CPD, WIDTH), BF16),
         vm((NLOC, FACES), BF16),
         vm((NLOC, OVL), F32),
         vm((CPD, FACES), BF16),
@@ -437,7 +465,7 @@
         vm((FACES, NRHS), F32),
         vm((CPD, NRHS), BF16),
         dma((STEPS, PARTS, 15)), dma((STEPS, PARTS, 15)),
-        dma((STEPS, PARTS, 15)), dma((STEPS, PARTS, 16)),
+        dma((STEPS, PARTS, 19)), dma((STEPS, PARTS, 21)),
         dma((2 * STEPS, PARTS, 4)), dma((2 * STEPS, PARTS, 4)),
         dma((len(args),)), dma((6,)),
     ]

time: 81.2 us -> 81 us (level); the launches traced: 80.1 us -> 80.9 us
  no operation moved by 1% of the time
where the time goes in v4:
time: 81 us; the launch traced here: 80.9 us
  Pallas kernels  80.1 us (99%)
    pallas_call x1, Pallas kernels, per_device(): pl.pallas_call(kernel, out_shape=handed_on, in_specs=[any_space] * len(ar...  78.8 us

profile of v4, /device:TPU:34, one launch (start us, length us, event | category | flops | bytes accessed | tf_op | source)
XLA Modules:
  0.0 80.9 jit_solution(14221530243092717905)
XLA Ops:
  0.6 78.8 %schwarz.1 = (f32[1024,256]{1,0:T(8,128)S(1)}, f32[1024,256]{1,0:T(8,128)S(1)}, bf16[2,512,128]{2,1,0:T(8,128)(2,1)S(1)}, bf16[1024,512]{1,0:T(8,128)(2,1)S(1)}, f32[1024,128]{1,0:T(8,128)S(1)}) custom-call(f32[1024,256]{1,0:T(8,128)} %rhs_h.1, bf16[1024,1024]{1,0:T(8,128)(2,1)} %lmat_h.1, bf16[1024,1024]{1,0:T(8,128)(2,1)} %linv_h.1, ...), custom_call_target="tpu_custom_call" | custom-call | tf_op jit(solution)/shard_map/schwarz/pallas_call | solution.py:480
  79.4 1.4 %last_residual.1 = (f32[1024,256]{1,0:T(8,128)}, f32[1024,256]{1,0:T(8,128)}) custom-call(f32[1024,256]{1,0:T(8,128)S(1)} %get-tuple-element.7.sol, f32[1024,256]{1,0:T(8,128)S(1)} %get-tuple-element.8.base, bf16[2,512,128]{2,1,0:T(8,128)(2,1)S(1)} %get-tuple-element.9.recv, bf16[1024,512]{1,0:T(8,128)(2,1)S(1)} %get-tuple-element.10.st, ...), custom_call_target="tpu_custom_call" | custom-call | tf_op jit(solution)/shard_map/last_residual/pallas_call | solution.py:491
